TPU v7x, 256 devices: a whole 4x4x8 slice. The times are simulated.
256 devices in a mesh: pairs: 32 (over y, z), tm: 8 (over x, core).
Axes of the slice: x: 4, y: 4, z: 8, core: 2. Of those that a mesh axis runs over, the one named last changes fastest.
Arguments:
- spectra: bfloat16 [8, 256, 2, 32768], P('tm', 'pairs'), may hold values from -6 to 6
- channel_slot: int32 [256], P('pairs'), may hold values from 0 to 7, as said below
- tile_list: int32 [63, 2], replicated, may hold values from 0 to 31, as said below
- tile_owner: int32 [63], replicated, may hold values from 0 to 31, as said below
Outputs:
- correlations: float32 [128, 64, 256], P('pairs', 'tm')
Inputs may be any that keep to these rules, and one draw needn't show every extreme that they name: `channel_slot`: within each block of 8 channels the values are a permutation of 0..7. `tile_list`: each row (i, j) has j = i or j = i + 1; every such pair of blocks appears exactly once, in some order. `tile_owner`: the owner of the tile in row p of tile_list is that row's i or i + 1; the tile of blocks 0 and 1 is owned by block 1; no owner holds more than 4 tiles, and some owner holds exactly 4.
All inputs are finite; a program needn't handle non-finite values.
Results may differ from a plain program's by a relative error of at most 0.00033.
Values may be sent and summed in bfloat16 or wider, within the bound.
A program may use at most 64 MiB of HBM per device.

v0:
```python
import math
import jax
import jax.numpy as jnp
from jax import lax
from jax.sharding import PartitionSpec as P

LAGS = 256
TILE_CAP = 4


def extended(block, sides, width):
    for axis, dim in sides:
        count = lax.axis_size(axis)
        forward = [(i, i + 1) for i in range(count - 1)]
        backward = [(target, source) for source, target in forward]
        low = lax.ppermute(
            lax.slice_in_dim(block, block.shape[dim] - width, None, axis=dim), axis, forward
        )
        high = lax.ppermute(lax.slice_in_dim(block, 0, width, axis=dim), axis, backward)
        block = jnp.concatenate([low, block, high], axis=dim)
    return block


def lag_table(freq_start, freq_width, bin_count, lag_count):
    freq_ids = freq_start + lax.iota(jnp.int32, freq_width)
    shift_lag = lax.iota(jnp.int32, lag_count) - lag_count // 2
    phase_steps = jnp.mod(freq_ids[:, None] * shift_lag[None, :], 2 * bin_count)
    phase_angle = phase_steps.astype(jnp.float32) * (math.pi / bin_count)
    cosine = jnp.cos(phase_angle).astype(jnp.bfloat16)
    sine_neg = (-jnp.sin(phase_angle)).astype(jnp.bfloat16)
    return jnp.concatenate([cosine, sine_neg], axis=0)


def cross_block(lead_block, tail_block):
    group_count = lead_block.shape[0]
    chan_count = lead_block.shape[1]
    lead_real = lead_block[:, :, 0].astype(jnp.float32)[:, :, None, :]
    lead_imag = lead_block[:, :, 1].astype(jnp.float32)[:, :, None, :]
    tail_real = tail_block[:, :, 0].astype(jnp.float32)[:, None, :, :]
    tail_imag = tail_block[:, :, 1].astype(jnp.float32)[:, None, :, :]
    real_part = lead_real * tail_real + lead_imag * tail_imag
    imag_part = lead_imag * tail_real - lead_real * tail_imag
    joined = jnp.concatenate(
        [real_part.astype(jnp.bfloat16), imag_part.astype(jnp.bfloat16)], axis=-1
    )
    return joined.reshape(group_count, chan_count * chan_count, joined.shape[-1])


def correlate(blocks, lead_pos, tail_pos, norm_scale):
    chan_count = blocks.shape[1]
    bin_count = blocks.shape[3]
    freq_width = min(2048, bin_count)
    slot_count = lead_pos.shape[0]

    def freq_turn(step_index, running):
        freq_start = step_index * freq_width
        freq_piece = lax.dynamic_slice_in_dim(blocks, freq_start, freq_width, 3)
        lead_block = jnp.take(freq_piece, lead_pos, axis=0)
        tail_block = jnp.take(freq_piece, tail_pos, axis=0)
        cross_spec = cross_block(lead_block, tail_block)
        lag_rows = lag_table(freq_start, freq_width, bin_count, LAGS)
        return running + jnp.einsum(
            "spf,fl->spl", cross_spec, lag_rows, preferred_element_type=jnp.float32
        )

    start_sum = jnp.zeros((slot_count, chan_count * chan_count, LAGS), jnp.float32)
    running = lax.fori_loop(0, bin_count // freq_width, freq_turn, start_sum)
    return running * norm_scale


def stack_windows(window_terms):
    summed = lax.psum(window_terms, "tm")
    share_rows = summed.shape[1] // lax.axis_size("tm")
    return lax.dynamic_slice_in_dim(summed, lax.axis_index("tm") * share_rows, share_rows, 1)


def on_device(spectra, channel_slot, tile_list, tile_owner):
    here_index = lax.axis_index("pairs")
    bin_count = spectra.shape[3]
    norm_scale = 1.0 / math.sqrt(2.0 * bin_count * lax.axis_size("tm"))
    ordered = jnp.take(spectra[0], channel_slot, axis=0)
    chan_count = ordered.shape[0]
    tile_count = tile_list.shape[0]
    low_block = tile_list[:, 0]
    high_block = tile_list[:, 1]
    earlier = lax.iota(jnp.int32, tile_count)[:, None] > lax.iota(jnp.int32, tile_count)[None, :]
    slot_rank = jnp.sum((tile_owner[:, None] == tile_owner[None, :]) & earlier, axis=1)
    slot_ids = lax.iota(jnp.int32, TILE_CAP)
    owned_slot = (
        (tile_owner[None, :] == here_index) & (slot_rank[None, :] == slot_ids[:, None])
    ).astype(jnp.int32)
    live_slot = jnp.sum(owned_slot, axis=1)
    slot_low = jnp.sum(owned_slot * low_block[None, :], axis=1)
    slot_high = jnp.sum(owned_slot * high_block[None, :], axis=1)
    widened = extended(ordered, (("pairs", 0),), chan_count)
    blocks = widened.reshape(3, chan_count, widened.shape[1], widened.shape[2])
    lead_pos = jnp.clip(slot_low - here_index + 1, 0, 2)
    tail_pos = jnp.clip(slot_high - here_index + 1, 0, 2)
    window_terms = correlate(blocks, lead_pos, tail_pos, norm_scale)
    window_terms = window_terms * live_slot[:, None, None].astype(jnp.float32)
    return stack_windows(window_terms)


def solution(mesh):
    placed = (P("tm", "pairs", None, None), P("pairs"), P(), P())
    return jax.shard_map(
        on_device, mesh=mesh, in_specs=placed, out_specs=P("pairs", "tm", None), check_vma=False
    )
```

profile of v0, /device:TPU:8, one launch (start us, length us, event | category | flops | bytes accessed | tf_op | source)
XLA Modules:
  0.0 379.8 jit_solution(1595996826397353993)
XLA Ops:
  8.0 2.7 gather_fusion.2
  11.6 7.7 %collective-permute-start.1 = (bf16[8,2,32768]{2,1,0:T(2,128)(2,1)S(1)}, bf16[8,2,32768]{2,1,0:T(2,128)(2,1)S(1)}, u32[]{:S(2)}, u32[]{:S(2)}) collective-permute-start(bf16[8,2,32768]{2,1,0:T(2,128)(2,1)S(1)} %broadcast_select_fusion.2), channel_id=1, source_target_pairs={{8,0},{16,8},{24,16},{32,24},{40,32},{48,40},{56,48},{64,56},{72,6... | collective-permute-start | bytes 3145736 | tf_op jit(solution)/shard_map/ppermute | solution.py:19
  19.3 1.9 collective-permute-start
  21.6 20.1 %collective-permute-done.1 = bf16[8,2,32768]{2,1,0:T(2,128)(2,1)S(1)} collective-permute-done((bf16[8,2,32768]{2,1,0:T(2,128)(2,1)S(1)}, bf16[8,2,32768]{2,1,0:T(2,128)(2,1)S(1)}, u32[]{:S(2)}, u32[]{:S(2)}) %collective-permute-start.1) | collective-permute-done | bytes 1048608 | tf_op jit(solution)/shard_map/ppermute | solution.py:19
  41.7 6.3 %collective-permute-done = bf16[8,2,32768]{2,1,0:T(2,128)(2,1)} collective-permute-done((bf16[8,2,32768]{2,1,0:T(2,128)(2,1)S(1)}, bf16[8,2,32768]{2,1,0:T(2,128)(2,1)}, u32[]{:S(2)}, u32[]{:S(2)}) %collective-permute-start) | collective-permute-done | bytes 1048608 | tf_op jit(solution)/shard_map/ppermute | solution.py:16
  48.0 7.1 %pad_maximum_fusion = bf16[24,2,32768]{2,1,0:T(2,128)(2,1)} fusion(bf16[8,2,32768]{2,1,0:T(2,128)(2,1)S(1)} %collective-permute-done.1, bf16[8,2,32768]{2,1,0:T(2,128)(2,1)S(1)} %broadcast_select_fusion.2, bf16[8,2,32768]{2,1,0:T(2,128)(2,1)} %collective-permute-done), kind=kLoop, calls=%fused_computation.45 | loop fusion | flops 3145728 | bytes 6291456 | tf_op jit(solution)/shard_map/concatenate | solution.py:20
  55.1 254.1 %while.16 = (s32[]{:T(128)}, f32[4,64,256]{2,1,0:T(8,128)S(1)}, bf16[3,8,2,32768]{3,2,1,0:T(2,128)(2,1)}, s32[4]{0:T(128)S(1)}, s32[4]{0:T(128)S(1)}, /*index=5*/s32[]{:T(128)}, s32[]{:T(128)}, s32[]{:T(128)}, s32[]{:T(128)}) while((s32[]{:T(128)}, f32[4,64,256]{2,1,0:T(8,128)S(1)}, bf16[3,8,2,32768]{3,2,1,0:T(2,128)(2,1)}, ...), condition=%wide.region_4.6_spmd.clone, body=%wide.region_3.5_spmd.clone.sunk | while | flops 559026496 | bytes 16148821 | solution.py:67
  55.2 1.1 constant_dynamic-slice_fusion.3
  56.3 1.1 gather_fusion.1
  57.7 1.1 gather_fusion
  60.7 9.4 %cosine_convert_fusion.2 = (bf16[2048,256]{1,0:T(8,128)(2,1)S(1)}, bf16[2048,256]{1,0:T(8,128)(2,1)S(1)}) fusion(s32[256]{0:T(256)S(1)} %iota_add_fusion.4, s32[2048]{0:T(1024)S(1)} %iota_add_fusion.5), kind=kLoop, calls=%fused_computation.19.clone.1 | loop fusion | flops 8912896 | bytes 2106368 | tf_op jit(solution)/shard_map/while/body/eval_jaxpr/convert_element_type | solution.py:29
  72.2 1.1 gather_fusion.1
  73.5 1.1 gather_fusion
  76.6 9.4 %cosine_convert_fusion.2 = (bf16[2048,256]{1,0:T(8,128)(2,1)S(1)}, bf16[2048,256]{1,0:T(8,128)(2,1)S(1)}) fusion(s32[256]{0:T(256)S(1)} %iota_add_fusion.4, s32[2048]{0:T(1024)S(1)} %iota_add_fusion.5), kind=kLoop, calls=%fused_computation.19.clone.1 | loop fusion | flops 8912896 | bytes 2106368 | tf_op jit(solution)/shard_map/while/body/eval_jaxpr/convert_element_type | solution.py:29
  87.0 1.1 constant_dynamic-slice_fusion.3
  88.0 1.1 gather_fusion.1
  89.4 1.1 gather_fusion
  92.5 9.4 %cosine_convert_fusion.2 = (bf16[2048,256]{1,0:T(8,128)(2,1)S(1)}, bf16[2048,256]{1,0:T(8,128)(2,1)S(1)}) fusion(s32[256]{0:T(256)S(1)} %iota_add_fusion.4, s32[2048]{0:T(1024)S(1)} %iota_add_fusion.5), kind=kLoop, calls=%fused_computation.19.clone.1 | loop fusion | flops 8912896 | bytes 2106368 | tf_op jit(solution)/shard_map/while/body/eval_jaxpr/convert_element_type | solution.py:29
  102.8 1.1 constant_dynamic-slice_fusion.3
  103.9 1.1 gather_fusion.1
  105.3 1.1 gather_fusion
  108.4 9.4 %cosine_convert_fusion.2 = (bf16[2048,256]{1,0:T(8,128)(2,1)S(1)}, bf16[2048,256]{1,0:T(8,128)(2,1)S(1)}) fusion(s32[256]{0:T(256)S(1)} %iota_add_fusion.4, s32[2048]{0:T(1024)S(1)} %iota_add_fusion.5), kind=kLoop, calls=%fused_computation.19.clone.1 | loop fusion | flops 8912896 | bytes 2106368 | tf_op jit(solution)/shard_map/while/body/eval_jaxpr/convert_element_type | solution.py:29
  118.7 1.1 constant_dynamic-slice_fusion.3
  119.8 1.1 gather_fusion.1
  121.2 1.1 gather_fusion
  124.2 9.4 %cosine_convert_fusion.2 = (bf16[2048,256]{1,0:T(8,128)(2,1)S(1)}, bf16[2048,256]{1,0:T(8,128)(2,1)S(1)}) fusion(s32[256]{0:T(256)S(1)} %iota_add_fusion.4, s32[2048]{0:T(1024)S(1)} %iota_add_fusion.5), kind=kLoop, calls=%fused_computation.19.clone.1 | loop fusion | flops 8912896 | bytes 2106368 | tf_op jit(solution)/shard_map/while/body/eval_jaxpr/convert_element_type | solution.py:29
  134.6 1.1 constant_dynamic-slice_fusion.3
  135.7 1.1 gather_fusion.1
  137.1 1.1 gather_fusion
  140.1 9.4 %cosine_convert_fusion.2 = (bf16[2048,256]{1,0:T(8,128)(2,1)S(1)}, bf16[2048,256]{1,0:T(8,128)(2,1)S(1)}) fusion(s32[256]{0:T(256)S(1)} %iota_add_fusion.4, s32[2048]{0:T(1024)S(1)} %iota_add_fusion.5), kind=kLoop, calls=%fused_computation.19.clone.1 | loop fusion | flops 8912896 | bytes 2106368 | tf_op jit(solution)/shard_map/while/body/eval_jaxpr/convert_element_type | solution.py:29
  150.5 1.1 constant_dynamic-slice_fusion.3
  151.6 1.1 gather_fusion.1
  152.9 1.1 gather_fusion
  156.0 9.4 %cosine_convert_fusion.2 = (bf16[2048,256]{1,0:T(8,128)(2,1)S(1)}, bf16[2048,256]{1,0:T(8,128)(2,1)S(1)}) fusion(s32[256]{0:T(256)S(1)} %iota_add_fusion.4, s32[2048]{0:T(1024)S(1)} %iota_add_fusion.5), kind=kLoop, calls=%fused_computation.19.clone.1 | loop fusion | flops 8912896 | bytes 2106368 | tf_op jit(solution)/shard_map/while/body/eval_jaxpr/convert_element_type | solution.py:29
  166.4 1.1 constant_dynamic-slice_fusion.3
  167.4 1.1 gather_fusion.1
  168.8 1.1 gather_fusion
  171.9 9.4 %cosine_convert_fusion.2 = (bf16[2048,256]{1,0:T(8,128)(2,1)S(1)}, bf16[2048,256]{1,0:T(8,128)(2,1)S(1)}) fusion(s32[256]{0:T(256)S(1)} %iota_add_fusion.4, s32[2048]{0:T(1024)S(1)} %iota_add_fusion.5), kind=kLoop, calls=%fused_computation.19.clone.1 | loop fusion | flops 8912896 | bytes 2106368 | tf_op jit(solution)/shard_map/while/body/eval_jaxpr/convert_element_type | solution.py:29
  183.3 1.1 gather_fusion.1
  184.7 1.1 gather_fusion
  187.8 9.4 %cosine_convert_fusion.2 = (bf16[2048,256]{1,0:T(8,128)(2,1)S(1)}, bf16[2048,256]{1,0:T(8,128)(2,1)S(1)}) fusion(s32[256]{0:T(256)S(1)} %iota_add_fusion.4, s32[2048]{0:T(1024)S(1)} %iota_add_fusion.5), kind=kLoop, calls=%fused_computation.19.clone.1 | loop fusion | flops 8912896 | bytes 2106368 | tf_op jit(solution)/shard_map/while/body/eval_jaxpr/convert_element_type | solution.py:29
  199.2 1.1 gather_fusion.1
  200.6 1.1 gather_fusion
  203.7 9.4 %cosine_convert_fusion.2 = (bf16[2048,256]{1,0:T(8,128)(2,1)S(1)}, bf16[2048,256]{1,0:T(8,128)(2,1)S(1)}) fusion(s32[256]{0:T(256)S(1)} %iota_add_fusion.4, s32[2048]{0:T(1024)S(1)} %iota_add_fusion.5), kind=kLoop, calls=%fused_computation.19.clone.1 | loop fusion | flops 8912896 | bytes 2106368 | tf_op jit(solution)/shard_map/while/body/eval_jaxpr/convert_element_type | solution.py:29
  215.1 1.1 gather_fusion.1
  216.5 1.1 gather_fusion
  219.5 9.4 %cosine_convert_fusion.2 = (bf16[2048,256]{1,0:T(8,128)(2,1)S(1)}, bf16[2048,256]{1,0:T(8,128)(2,1)S(1)}) fusion(s32[256]{0:T(256)S(1)} %iota_add_fusion.4, s32[2048]{0:T(1024)S(1)} %iota_add_fusion.5), kind=kLoop, calls=%fused_computation.19.clone.1 | loop fusion | flops 8912896 | bytes 2106368 | tf_op jit(solution)/shard_map/while/body/eval_jaxpr/convert_element_type | solution.py:29
  231.0 1.1 gather_fusion.1
  232.4 1.1 gather_fusion
  235.4 9.4 %cosine_convert_fusion.2 = (bf16[2048,256]{1,0:T(8,128)(2,1)S(1)}, bf16[2048,256]{1,0:T(8,128)(2,1)S(1)}) fusion(s32[256]{0:T(256)S(1)} %iota_add_fusion.4, s32[2048]{0:T(1024)S(1)} %iota_add_fusion.5), kind=kLoop, calls=%fused_computation.19.clone.1 | loop fusion | flops 8912896 | bytes 2106368 | tf_op jit(solution)/shard_map/while/body/eval_jaxpr/convert_element_type | solution.py:29
  246.9 1.1 gather_fusion.1
  248.2 1.1 gather_fusion
  251.3 9.4 %cosine_convert_fusion.2 = (bf16[2048,256]{1,0:T(8,128)(2,1)S(1)}, bf16[2048,256]{1,0:T(8,128)(2,1)S(1)}) fusion(s32[256]{0:T(256)S(1)} %iota_add_fusion.4, s32[2048]{0:T(1024)S(1)} %iota_add_fusion.5), kind=kLoop, calls=%fused_computation.19.clone.1 | loop fusion | flops 8912896 | bytes 2106368 | tf_op jit(solution)/shard_map/while/body/eval_jaxpr/convert_element_type | solution.py:29
  262.7 1.1 gather_fusion.1
  264.1 1.1 gather_fusion
  267.2 9.4 %cosine_convert_fusion.2 = (bf16[2048,256]{1,0:T(8,128)(2,1)S(1)}, bf16[2048,256]{1,0:T(8,128)(2,1)S(1)}) fusion(s32[256]{0:T(256)S(1)} %iota_add_fusion.4, s32[2048]{0:T(1024)S(1)} %iota_add_fusion.5), kind=kLoop, calls=%fused_computation.19.clone.1 | loop fusion | flops 8912896 | bytes 2106368 | tf_op jit(solution)/shard_map/while/body/eval_jaxpr/convert_element_type | solution.py:29
  278.6 1.1 gather_fusion.1
  280.0 1.1 gather_fusion
  283.1 9.4 %cosine_convert_fusion.2 = (bf16[2048,256]{1,0:T(8,128)(2,1)S(1)}, bf16[2048,256]{1,0:T(8,128)(2,1)S(1)}) fusion(s32[256]{0:T(256)S(1)} %iota_add_fusion.4, s32[2048]{0:T(1024)S(1)} %iota_add_fusion.5), kind=kLoop, calls=%fused_computation.19.clone.1 | loop fusion | flops 8912896 | bytes 2106368 | tf_op jit(solution)/shard_map/while/body/eval_jaxpr/convert_element_type | solution.py:29
  294.5 1.1 gather_fusion.1
  295.9 1.1 gather_fusion
  299.0 9.4 %cosine_convert_fusion.2 = (bf16[2048,256]{1,0:T(8,128)(2,1)S(1)}, bf16[2048,256]{1,0:T(8,128)(2,1)S(1)}) fusion(s32[256]{0:T(256)S(1)} %iota_add_fusion.4, s32[2048]{0:T(1024)S(1)} %iota_add_fusion.5), kind=kLoop, calls=%fused_computation.19.clone.1 | loop fusion | flops 8912896 | bytes 2106368 | tf_op jit(solution)/shard_map/while/body/eval_jaxpr/convert_element_type | solution.py:29
  310.0 61.6 %all-reduce.2.cloned.1.call-done = f32[4,64,256]{2,1,0:T(8,128)} async-done(((f32[4,64,256]{2,1,0:T(8,128)}), f32[4,64,256]{2,1,0:T(8,128)}) %all-reduce.2.cloned.1.call-update) | async-done | bytes 262160 | tf_op jit(solution)/shard_map/psum | solution.py:72
  371.6 1.4 constant_dynamic-slice_fusion.1
  (285 shorter events, 62.3 us)
Async XLA Ops:
  6.5 1.4 copy-start
  6.5 365.1 %all-reduce.2.cloned.1.call-start = ((), (), s32[]{:S(2)}) async-start(), calls=%async_computation | async-start | bytes 524288 | tf_op jit(solution)/shard_map/psum | solution.py:72
  8.0 13.3 %copy-start.2 = (s32[63]{0:T(128)S(1)}, s32[63]{0:T(128)}, u32[]{:S(2)}) copy-start(s32[63]{0:T(128)} %param.11) | copy-start | bytes 760
  8.0 13.5 %copy-start.1 = (s32[63,2]{0,1:T(2,128)S(1)}, s32[63,2]{0,1:T(2,128)}, u32[]{:S(2)}) copy-start(s32[63,2]{0,1:T(2,128)} %param.10) | copy-start | bytes 1516
  11.6 30.1 %collective-permute-start.1 = (bf16[8,2,32768]{2,1,0:T(2,128)(2,1)S(1)}, bf16[8,2,32768]{2,1,0:T(2,128)(2,1)S(1)}, u32[]{:S(2)}, u32[]{:S(2)}) collective-permute-start(bf16[8,2,32768]{2,1,0:T(2,128)(2,1)S(1)} %broadcast_select_fusion.2), channel_id=1, source_target_pairs={{8,0},{16,8},{24,16},{32,24},{40,32},{48,40},{56,48},{64,56},{72,6... | collective-permute-start | bytes 3145736 | tf_op jit(solution)/shard_map/ppermute | solution.py:19
  19.3 28.7 %collective-permute-start = (bf16[8,2,32768]{2,1,0:T(2,128)(2,1)S(1)}, bf16[8,2,32768]{2,1,0:T(2,128)(2,1)}, u32[]{:S(2)}, u32[]{:S(2)}) collective-permute-start(bf16[8,2,32768]{2,1,0:T(2,128)(2,1)S(1)} %broadcast_select_fusion.2), channel_id=1, source_target_pairs={{0,8},{8,16},{16,24},{24,32},{32,40},{40,48},{48,56},{56,64},{64,7... | collective-permute-start | bytes 3145736 | tf_op jit(solution)/shard_map/ppermute | solution.py:16
Sparse Core Ops, SparseCore 0:
  310.1 61.4 all-reduce.1
where the time goes:
time: 381 us; the launch traced here: 380 us
  other arithmetic  192 us (50%)
  waiting for transfers between devices  88 us (23%)
  local copies, waits for them, and re-layouts  60.9 us (16%)
  between operations  13.5 us (4%)
  matrix products  12.9 us (3%)
  starting transfers between devices  9.57 us (3%)
    convert_element_type x16, other arithmetic, lag_table(): cosine = jnp.cos(phase_angle).astype(jnp.bfloat16)  151 us
    psum x1, waiting for transfers between devices, stack_windows(): summed = lax.psum(window_terms, 'tm')  61.6 us
    ppermute x1, waiting for transfers between devices, extended(): lax.ppermute(lax.slice_in_dim(block, 0, width, axis=dim), axis, backward)  20.1 us
    gather x16, local copies, waits for them, and re-layouts, freq_turn(): tail_block = jnp.take(freq_piece, tail_pos, axis=0)  17.2 us
    gather x16, local copies, waits for them, and re-layouts, freq_turn(): lead_block = jnp.take(freq_piece, lead_pos, axis=0)  17.2 us
    dynamic_slice x16, local copies, waits for them, and re-layouts, freq_turn(): freq_piece = lax.dynamic_slice_in_dim(blocks, freq_start, freq_width, 3)  17.1 us
    dot_general x16, matrix products, freq_turn(): jnp.einsum('spf,fl->spl', cross_spec, lag_rows, preferred_element_type=jn...  12.9 us
    convert_element_type x16, other arithmetic, cross_block(): real_part.astype(jnp.bfloat16)  8.57 us
  transfers between devices with their start and end apart: 3, of which 3 were waited for; matrix products, arithmetic and copies ran while one was open for 0% of the time, Pallas kernels for 0%

commit v1 on v0

--- a/solution.py
+++ b/solution.py
@@ -69,7 +69,17 @@
 
 
 def stack_windows(window_terms):
-    summed = lax.psum(window_terms, "tm")
+
+    def wait_members_all(x_in):
+        axis_tag = "tm"
+        q_n = jax.lax.axis_size(axis_tag)
+        response = lambda e_next: [(s, s ^ e_next) for s in range(q_n)]
+        t_next = x_in
+        for j in range(q_n.bit_length() - 1):
+            t_next = t_next + jax.lax.ppermute(t_next, axis_name=axis_tag, perm=response(1 << j))
+        return t_next
+
+    summed = wait_members_all(window_terms)
     share_rows = summed.shape[1] // lax.axis_size("tm")
     return lax.dynamic_slice_in_dim(summed, lax.axis_index("tm") * share_rows, share_rows, 1)
 

time: 381 us -> 324 us (0.85)
  waiting for transfers between devices: 88 us -> 40.6 us
  between operations: 13.5 us -> 0.13 us
  starting transfers between devices: 9.57 us -> 14.5 us
    psum x1 -> x0, waiting for transfers between devices: 61.6 us -> none  [stack_windows(): summed = lax.psum(window_terms, 'tm')]
    ppermute x0 -> x3, waiting for transfers between devices: none -> 14.2 us  [wait_members_all(): jax.lax.ppermute(t_next, axis_name=axis_tag, perm=response(1 << j))]
    ppermute x0 -> x3, starting transfers between devices: none -> 4.92 us  [wait_members_all(): jax.lax.ppermute(t_next, axis_name=axis_tag, perm=response(1 << j))]
  transfers between devices with their start and end apart: 3 -> 5, of which waited for: 3 -> 5; matrix products, arithmetic and copies ran while one was open for 0% -> 0% of each run, Pallas kernels for 0% -> 0%
where the time goes in v1:
time: 324 us; the launch traced here: 323 us
  other arithmetic  193 us (60%)
  local copies, waits for them, and re-layouts  59.6 us (18%)
  waiting for transfers between devices  40.6 us (13%)
  starting transfers between devices  14.5 us (4%)
  matrix products  12.9 us (4%)
    convert_element_type x16, other arithmetic, lag_table(): cosine = jnp.cos(phase_angle).astype(jnp.bfloat16)  151 us
    ppermute x1, waiting for transfers between devices, extended(): lax.ppermute(lax.slice_in_dim(block, 0, width, axis=dim), axis, backward)  20.1 us
    gather x16, local copies, waits for them, and re-layouts, freq_turn(): lead_block = jnp.take(freq_piece, lead_pos, axis=0)  17.2 us
    gather x16, local copies, waits for them, and re-layouts, freq_turn(): tail_block = jnp.take(freq_piece, tail_pos, axis=0)  17.2 us
    dynamic_slice x16, local copies, waits for them, and re-layouts, freq_turn(): freq_piece = lax.dynamic_slice_in_dim(blocks, freq_start, freq_width, 3)  17.1 us
    ppermute x3, waiting for transfers between devices, wait_members_all(): jax.lax.ppermute(t_next, axis_name=axis_tag, perm=response(1 << j))  14.2 us
    dot_general x16, matrix products, freq_turn(): jnp.einsum('spf,fl->spl', cross_spec, lag_rows, preferred_element_type=jn...  12.9 us
    convert_element_type x16, other arithmetic, cross_block(): real_part.astype(jnp.bfloat16)  8.99 us
  transfers between devices with their start and end apart: 5, of which 5 were waited for; matrix products, arithmetic and copies ran while one was open for 0% of the time, Pallas kernels for 0%

profile of v1, /device:TPU:8, one launch (start us, length us, event | category | flops | bytes accessed | tf_op | source)
XLA Modules:
  0.0 323.4 jit_solution(16982035964474105984)
XLA Ops:
  1.4 2.7 gather_fusion.2
  5.1 7.7 %collective-permute-start.1 = (bf16[8,2,32768]{2,1,0:T(2,128)(2,1)S(1)}, bf16[8,2,32768]{2,1,0:T(2,128)(2,1)}, u32[]{:S(2)}, u32[]{:S(2)}) collective-permute-start(bf16[8,2,32768]{2,1,0:T(2,128)(2,1)S(1)} %broadcast_select_fusion.2), channel_id=1, source_target_pairs={{8,0},{16,8},{24,16},{32,24},{40,32},{48,40},{56,48},{64,56},{72,6... | collective-permute-start | bytes 3145736 | tf_op jit(solution)/shard_map/ppermute | solution.py:19
  12.7 1.9 collective-permute-start
  15.1 20.1 %collective-permute-done.1 = bf16[8,2,32768]{2,1,0:T(2,128)(2,1)} collective-permute-done((bf16[8,2,32768]{2,1,0:T(2,128)(2,1)S(1)}, bf16[8,2,32768]{2,1,0:T(2,128)(2,1)}, u32[]{:S(2)}, u32[]{:S(2)}) %collective-permute-start.1) | collective-permute-done | bytes 1048608 | tf_op jit(solution)/shard_map/ppermute | solution.py:19
  35.1 6.3 %collective-permute-done = bf16[8,2,32768]{2,1,0:T(2,128)(2,1)} collective-permute-done((bf16[8,2,32768]{2,1,0:T(2,128)(2,1)S(1)}, bf16[8,2,32768]{2,1,0:T(2,128)(2,1)}, u32[]{:S(2)}, u32[]{:S(2)}) %collective-permute-start) | collective-permute-done | bytes 1048608 | tf_op jit(solution)/shard_map/ppermute | solution.py:16
  41.5 7.4 %pad_maximum_fusion = bf16[24,2,32768]{2,1,0:T(2,128)(2,1)} fusion(bf16[8,2,32768]{2,1,0:T(2,128)(2,1)} %collective-permute-done.1, bf16[8,2,32768]{2,1,0:T(2,128)(2,1)S(1)} %broadcast_select_fusion.2, bf16[8,2,32768]{2,1,0:T(2,128)(2,1)} %collective-permute-done), kind=kLoop, calls=%fused_computation.45 | loop fusion | flops 3145728 | bytes 6291456 | tf_op jit(solution)/shard_map/concatenate | solution.py:20
  48.9 254.5 %while.16 = (s32[]{:T(128)}, f32[4,64,256]{2,1,0:T(8,128)S(1)}, bf16[3,8,2,32768]{3,2,1,0:T(2,128)(2,1)}, s32[4]{0:T(128)S(1)}, s32[4]{0:T(128)S(1)}, /*index=5*/s32[]{:T(128)}, s32[]{:T(128)}, s32[]{:T(128)}, s32[]{:T(128)}) while((s32[]{:T(128)}, f32[4,64,256]{2,1,0:T(8,128)S(1)}, bf16[3,8,2,32768]{3,2,1,0:T(2,128)(2,1)}, ...), condition=%wide.region_4.6_spmd.clone, body=%wide.region_3.5_spmd.clone.sunk | while | flops 559026496 | bytes 16148821 | solution.py:67
  49.0 1.1 constant_dynamic-slice_fusion.2
  50.0 1.1 gather_fusion.1
  51.4 1.1 gather_fusion
  54.5 9.4 %cosine_convert_fusion.2 = (bf16[2048,256]{1,0:T(8,128)(2,1)S(1)}, bf16[2048,256]{1,0:T(8,128)(2,1)S(1)}) fusion(s32[256]{0:T(256)S(1)} %iota_add_fusion.4, s32[2048]{0:T(1024)S(1)} %iota_add_fusion.5), kind=kLoop, calls=%fused_computation.19.clone.1 | loop fusion | flops 8912896 | bytes 2106368 | tf_op jit(solution)/shard_map/while/body/eval_jaxpr/convert_element_type | solution.py:29
  65.9 1.1 gather_fusion.1
  67.3 1.1 gather_fusion
  70.4 9.4 %cosine_convert_fusion.2 = (bf16[2048,256]{1,0:T(8,128)(2,1)S(1)}, bf16[2048,256]{1,0:T(8,128)(2,1)S(1)}) fusion(s32[256]{0:T(256)S(1)} %iota_add_fusion.4, s32[2048]{0:T(1024)S(1)} %iota_add_fusion.5), kind=kLoop, calls=%fused_computation.19.clone.1 | loop fusion | flops 8912896 | bytes 2106368 | tf_op jit(solution)/shard_map/while/body/eval_jaxpr/convert_element_type | solution.py:29
  81.8 1.1 gather_fusion.1
  83.2 1.1 gather_fusion
  86.3 9.4 %cosine_convert_fusion.2 = (bf16[2048,256]{1,0:T(8,128)(2,1)S(1)}, bf16[2048,256]{1,0:T(8,128)(2,1)S(1)}) fusion(s32[256]{0:T(256)S(1)} %iota_add_fusion.4, s32[2048]{0:T(1024)S(1)} %iota_add_fusion.5), kind=kLoop, calls=%fused_computation.19.clone.1 | loop fusion | flops 8912896 | bytes 2106368 | tf_op jit(solution)/shard_map/while/body/eval_jaxpr/convert_element_type | solution.py:29
  96.7 1.1 constant_dynamic-slice_fusion.2
  97.8 1.1 gather_fusion.1
  99.1 1.1 gather_fusion
  102.2 9.4 %cosine_convert_fusion.2 = (bf16[2048,256]{1,0:T(8,128)(2,1)S(1)}, bf16[2048,256]{1,0:T(8,128)(2,1)S(1)}) fusion(s32[256]{0:T(256)S(1)} %iota_add_fusion.4, s32[2048]{0:T(1024)S(1)} %iota_add_fusion.5), kind=kLoop, calls=%fused_computation.19.clone.1 | loop fusion | flops 8912896 | bytes 2106368 | tf_op jit(solution)/shard_map/while/body/eval_jaxpr/convert_element_type | solution.py:29
  112.6 1.1 constant_dynamic-slice_fusion.2
  113.7 1.1 gather_fusion.1
  115.0 1.1 gather_fusion
  118.1 9.4 %cosine_convert_fusion.2 = (bf16[2048,256]{1,0:T(8,128)(2,1)S(1)}, bf16[2048,256]{1,0:T(8,128)(2,1)S(1)}) fusion(s32[256]{0:T(256)S(1)} %iota_add_fusion.4, s32[2048]{0:T(1024)S(1)} %iota_add_fusion.5), kind=kLoop, calls=%fused_computation.19.clone.1 | loop fusion | flops 8912896 | bytes 2106368 | tf_op jit(solution)/shard_map/while/body/eval_jaxpr/convert_element_type | solution.py:29
  129.6 1.1 gather_fusion.1
  131.0 1.1 gather_fusion
  134.0 9.4 %cosine_convert_fusion.2 = (bf16[2048,256]{1,0:T(8,128)(2,1)S(1)}, bf16[2048,256]{1,0:T(8,128)(2,1)S(1)}) fusion(s32[256]{0:T(256)S(1)} %iota_add_fusion.4, s32[2048]{0:T(1024)S(1)} %iota_add_fusion.5), kind=kLoop, calls=%fused_computation.19.clone.1 | loop fusion | flops 8912896 | bytes 2106368 | tf_op jit(solution)/shard_map/while/body/eval_jaxpr/convert_element_type | solution.py:29
  144.4 1.1 constant_dynamic-slice_fusion.2
  145.5 1.1 gather_fusion.1
  146.9 1.1 gather_fusion
  150.0 9.4 %cosine_convert_fusion.2 = (bf16[2048,256]{1,0:T(8,128)(2,1)S(1)}, bf16[2048,256]{1,0:T(8,128)(2,1)S(1)}) fusion(s32[256]{0:T(256)S(1)} %iota_add_fusion.4, s32[2048]{0:T(1024)S(1)} %iota_add_fusion.5), kind=kLoop, calls=%fused_computation.19.clone.1 | loop fusion | flops 8912896 | bytes 2106368 | tf_op jit(solution)/shard_map/while/body/eval_jaxpr/convert_element_type | solution.py:29
  161.4 1.1 gather_fusion.1
  162.8 1.1 gather_fusion
  165.9 9.4 %cosine_convert_fusion.2 = (bf16[2048,256]{1,0:T(8,128)(2,1)S(1)}, bf16[2048,256]{1,0:T(8,128)(2,1)S(1)}) fusion(s32[256]{0:T(256)S(1)} %iota_add_fusion.4, s32[2048]{0:T(1024)S(1)} %iota_add_fusion.5), kind=kLoop, calls=%fused_computation.19.clone.1 | loop fusion | flops 8912896 | bytes 2106368 | tf_op jit(solution)/shard_map/while/body/eval_jaxpr/convert_element_type | solution.py:29
  177.3 1.1 gather_fusion.1
  178.7 1.1 gather_fusion
  181.8 9.4 %cosine_convert_fusion.2 = (bf16[2048,256]{1,0:T(8,128)(2,1)S(1)}, bf16[2048,256]{1,0:T(8,128)(2,1)S(1)}) fusion(s32[256]{0:T(256)S(1)} %iota_add_fusion.4, s32[2048]{0:T(1024)S(1)} %iota_add_fusion.5), kind=kLoop, calls=%fused_computation.19.clone.1 | loop fusion | flops 8912896 | bytes 2106368 | tf_op jit(solution)/shard_map/while/body/eval_jaxpr/convert_element_type | solution.py:29
  193.2 1.1 gather_fusion.1
  194.6 1.1 gather_fusion
  197.7 9.4 %cosine_convert_fusion.2 = (bf16[2048,256]{1,0:T(8,128)(2,1)S(1)}, bf16[2048,256]{1,0:T(8,128)(2,1)S(1)}) fusion(s32[256]{0:T(256)S(1)} %iota_add_fusion.4, s32[2048]{0:T(1024)S(1)} %iota_add_fusion.5), kind=kLoop, calls=%fused_computation.19.clone.1 | loop fusion | flops 8912896 | bytes 2106368 | tf_op jit(solution)/shard_map/while/body/eval_jaxpr/convert_element_type | solution.py:29
  209.1 1.1 gather_fusion.1
  210.5 1.1 gather_fusion
  213.6 9.4 %cosine_convert_fusion.2 = (bf16[2048,256]{1,0:T(8,128)(2,1)S(1)}, bf16[2048,256]{1,0:T(8,128)(2,1)S(1)}) fusion(s32[256]{0:T(256)S(1)} %iota_add_fusion.4, s32[2048]{0:T(1024)S(1)} %iota_add_fusion.5), kind=kLoop, calls=%fused_computation.19.clone.1 | loop fusion | flops 8912896 | bytes 2106368 | tf_op jit(solution)/shard_map/while/body/eval_jaxpr/convert_element_type | solution.py:29
  225.0 1.1 gather_fusion.1
  226.4 1.1 gather_fusion
  229.5 9.4 %cosine_convert_fusion.2 = (bf16[2048,256]{1,0:T(8,128)(2,1)S(1)}, bf16[2048,256]{1,0:T(8,128)(2,1)S(1)}) fusion(s32[256]{0:T(256)S(1)} %iota_add_fusion.4, s32[2048]{0:T(1024)S(1)} %iota_add_fusion.5), kind=kLoop, calls=%fused_computation.19.clone.1 | loop fusion | flops 8912896 | bytes 2106368 | tf_op jit(solution)/shard_map/while/body/eval_jaxpr/convert_element_type | solution.py:29
  240.9 1.1 gather_fusion.1
  242.3 1.1 gather_fusion
  245.4 9.4 %cosine_convert_fusion.2 = (bf16[2048,256]{1,0:T(8,128)(2,1)S(1)}, bf16[2048,256]{1,0:T(8,128)(2,1)S(1)}) fusion(s32[256]{0:T(256)S(1)} %iota_add_fusion.4, s32[2048]{0:T(1024)S(1)} %iota_add_fusion.5), kind=kLoop, calls=%fused_computation.19.clone.1 | loop fusion | flops 8912896 | bytes 2106368 | tf_op jit(solution)/shard_map/while/body/eval_jaxpr/convert_element_type | solution.py:29
  256.8 1.1 gather_fusion.1
  258.2 1.1 gather_fusion
  261.3 9.4 %cosine_convert_fusion.2 = (bf16[2048,256]{1,0:T(8,128)(2,1)S(1)}, bf16[2048,256]{1,0:T(8,128)(2,1)S(1)}) fusion(s32[256]{0:T(256)S(1)} %iota_add_fusion.4, s32[2048]{0:T(1024)S(1)} %iota_add_fusion.5), kind=kLoop, calls=%fused_computation.19.clone.1 | loop fusion | flops 8912896 | bytes 2106368 | tf_op jit(solution)/shard_map/while/body/eval_jaxpr/convert_element_type | solution.py:29
  272.7 1.1 gather_fusion.1
  274.1 1.1 gather_fusion
  277.2 9.4 %cosine_convert_fusion.2 = (bf16[2048,256]{1,0:T(8,128)(2,1)S(1)}, bf16[2048,256]{1,0:T(8,128)(2,1)S(1)}) fusion(s32[256]{0:T(256)S(1)} %iota_add_fusion.4, s32[2048]{0:T(1024)S(1)} %iota_add_fusion.5), kind=kLoop, calls=%fused_computation.19.clone.1 | loop fusion | flops 8912896 | bytes 2106368 | tf_op jit(solution)/shard_map/while/body/eval_jaxpr/convert_element_type | solution.py:29
  288.6 1.1 gather_fusion.1
  290.0 1.1 gather_fusion
  293.1 9.4 %cosine_convert_fusion.2 = (bf16[2048,256]{1,0:T(8,128)(2,1)S(1)}, bf16[2048,256]{1,0:T(8,128)(2,1)S(1)}) fusion(s32[256]{0:T(256)S(1)} %iota_add_fusion.4, s32[2048]{0:T(1024)S(1)} %iota_add_fusion.5), kind=kLoop, calls=%fused_computation.19.clone.1 | loop fusion | flops 8912896 | bytes 2106368 | tf_op jit(solution)/shard_map/while/body/eval_jaxpr/convert_element_type | solution.py:29
  303.6 1.5 collective-permute-done.2
  305.2 1.6 collective-permute-start.3
  306.8 6.8 %collective-permute-done.3 = f32[4,64,256]{2,1,0:T(8,128)S(1)} collective-permute-done((f32[4,64,256]{2,1,0:T(8,128)S(1)}, f32[4,64,256]{2,1,0:T(8,128)S(1)}, u32[]{:S(2)}, u32[]{:S(2)}) %collective-permute-start.3) | collective-permute-done | bytes 262176 | tf_op jit(solution)/shard_map/ppermute | solution.py:79
  313.7 3.2 collective-permute-start.4
  316.9 5.9 %collective-permute-done.4 = f32[4,64,256]{2,1,0:T(8,128)S(1)} collective-permute-done((f32[4,64,256]{2,1,0:T(8,128)S(1)}, f32[4,64,256]{2,1,0:T(8,128)S(1)}, u32[]{:S(2)}, u32[]{:S(2)}) %collective-permute-start.4) | collective-permute-done | bytes 262176 | tf_op jit(solution)/shard_map/ppermute | solution.py:79
  (290 shorter events, 66.1 us)
Async XLA Ops:
  0.0 1.4 copy-start
  1.4 13.3 %copy-start.2 = (s32[63]{0:T(128)S(1)}, s32[63]{0:T(128)}, u32[]{:S(2)}) copy-start(s32[63]{0:T(128)} %param.11) | copy-start | bytes 760
  1.4 13.5 %copy-start.1 = (s32[63,2]{0,1:T(2,128)S(1)}, s32[63,2]{0,1:T(2,128)}, u32[]{:S(2)}) copy-start(s32[63,2]{0,1:T(2,128)} %param.10) | copy-start | bytes 1516
  5.1 30.1 %collective-permute-start.1 = (bf16[8,2,32768]{2,1,0:T(2,128)(2,1)S(1)}, bf16[8,2,32768]{2,1,0:T(2,128)(2,1)}, u32[]{:S(2)}, u32[]{:S(2)}) collective-permute-start(bf16[8,2,32768]{2,1,0:T(2,128)(2,1)S(1)} %broadcast_select_fusion.2), channel_id=1, source_target_pairs={{8,0},{16,8},{24,16},{32,24},{40,32},{48,40},{56,48},{64,56},{72,6... | collective-permute-start | bytes 3145736 | tf_op jit(solution)/shard_map/ppermute | solution.py:19
  12.7 28.7 %collective-permute-start = (bf16[8,2,32768]{2,1,0:T(2,128)(2,1)S(1)}, bf16[8,2,32768]{2,1,0:T(2,128)(2,1)}, u32[]{:S(2)}, u32[]{:S(2)}) collective-permute-start(bf16[8,2,32768]{2,1,0:T(2,128)(2,1)S(1)} %broadcast_select_fusion.2), channel_id=1, source_target_pairs={{0,8},{8,16},{16,24},{24,32},{32,40},{40,48},{48,56},{56,64},{64,7... | collective-permute-start | bytes 3145736 | tf_op jit(solution)/shard_map/ppermute | solution.py:16
  303.5 1.6 collective-permute-start.2
  305.2 8.4 %collective-permute-start.3 = (f32[4,64,256]{2,1,0:T(8,128)S(1)}, f32[4,64,256]{2,1,0:T(8,128)S(1)}, u32[]{:S(2)}, u32[]{:S(2)}) collective-permute-start(f32[4,64,256]{2,1,0:T(8,128)S(1)} %fusion.17), channel_id=1, source_target_pairs={{0,2},{1,3},{2,0},{3,1},{4,6},{5,7},{6,4},{7,5},{8,10},{9,11},{10,... | collective-permute-start | bytes 786440 | tf_op jit(solution)/shard_map/ppermute | solution.py:79
  313.7 9.1 %collective-permute-start.4 = (f32[4,64,256]{2,1,0:T(8,128)S(1)}, f32[4,64,256]{2,1,0:T(8,128)S(1)}, u32[]{:S(2)}, u32[]{:S(2)}) collective-permute-start(f32[4,64,256]{2,1,0:T(8,128)S(1)} %add.123), channel_id=1, source_target_pairs={{0,4},{1,5},{2,6},{3,7},{4,0},{5,1},{6,2},{7,3},{8,12},{9,13},{10,... | collective-permute-start | bytes 786440 | tf_op jit(solution)/shard_map/ppermute | solution.py:79
